TPU v7x, 32 devices: a whole 2x2x4 slice. The times are simulated.
32 devices in a mesh: groups: 2 (over x), seq: 16 (over z, y, core).
Axes of the slice: x: 2, y: 2, z: 4, core: 2. Of those that a mesh axis runs over, the one named last changes fastest.
Arguments:
- queries: bfloat16 [8192, 1280], P(('groups', 'seq')), parts along dimension 0, may hold values from -6 to 6
- keys: bfloat16 [8192, 1280], P(('groups', 'seq')), parts along dimension 0, may hold values from -6 to 6
- values: bfloat16 [8192, 1280], P(('groups', 'seq')), parts along dimension 0, may hold values from -6 to 6
- cotangent: bfloat16 [8192, 1280], P(('groups', 'seq')), parts along dimension 0, may hold values from -6 to 6
- local_blocks: int32 [64, 3], P('groups'), parts along dimension 0, may hold values from -1 to 31, as said below
- far_blocks: int32 [64, 4], P('groups'), parts along dimension 0, may hold values from -1 to 29, as said below
- counts: int32 [64], P('groups'), parts along dimension 0, may hold values from 2 to 128
Outputs:
- attended: bfloat16 [8192, 1280], P(('groups', 'seq')), parts along dimension 0
- grad_queries: bfloat16 [8192, 1280], P(('groups', 'seq')), parts along dimension 0
- grad_keys: bfloat16 [8192, 1280], P(('groups', 'seq')), parts along dimension 0
- grad_values: bfloat16 [8192, 1280], P(('groups', 'seq')), parts along dimension 0
There are 2 independent parts, one for each index of `groups`. A program takes and returns all parts, laid end to end along the dimension named above; each array names one. Nothing has to cross between parts.
Inputs may be any that keep to these rules, and one draw needn't show every extreme that they name: `local_blocks`: row b holds block b itself first, then 3 - 1 distinct blocks whose index differs from b by 1 to 2, or -1 where such a block lies outside the sequence. `far_blocks`: each entry of row b is -1 or a block whose index lies in [(b // 2 - k) * 2, (b // 2 - k + 1) * 2) for some k from 1 to 2; it is -1 exactly where that range would start below 0. Entries may repeat.
All inputs are finite; a program needn't handle non-finite values.
Results may differ from a plain program's by a relative error of at most 0.027.
Values may be sent and summed in bfloat16 or wider, within the bound.
A program may use at most 128 MiB of HBM per device.

v0:
```python
import functools
import math

import jax
import jax.numpy as jnp
from jax import lax
from jax.experimental import pallas as pl
from jax.experimental.pallas import tpu as pltpu
from jax.sharding import PartitionSpec as P

HEADS = 16
BLK = 128
MESH = pl.DeviceIdType.MESH
OFF = -1e30
NCH = 2
BF = jnp.bfloat16
F32 = jnp.float32


def dot_nt(a, b):
    return lax.dot_general(a, b, (((1,), (1,)), ((), ())), preferred_element_type=F32)


def dot_nn(a, b):
    return lax.dot_general(a, b, (((1,), (0,)), ((), ())), preferred_element_type=F32)


def dot_tn(a, b):
    return lax.dot_general(a, b, (((0,), (0,)), ((), ())), preferred_element_type=F32)


def kernel(
    n, q_hbm, k_hbm, v_hbm, g_hbm, local_ref, far_ref, counts_ref,
    o_ref, dq_ref, dk_ref, dv_ref,
    kbuf, vbuf, qbuf, gbuf, bias, acc, own, oacc, gsend, grecv,
    own_sem, kv_send, kv_recv, gr_send, gr_recv,
):
    d = lax.axis_index("seq")
    even = lax.rem(d, 2) == 0
    rows, width = q_hbm.shape
    cols = width // NCH
    head = width // HEADS
    hpc = HEADS // NCH
    blocks = rows // BLK
    nblk = counts_ref.shape[0]
    hbm = (k_hbm, v_hbm)
    bufs = (kbuf, vbuf)
    scale = 1.0 / math.sqrt(head)

    def part(ref, c):
        return ref.at[:, pl.ds(pl.multiple_of(c * cols, 128), cols)]

    def slot(a, c, s):
        return bufs[a].at[c, pl.ds(s * rows, rows), :]

    def own_copies(c):
        out = []
        for i, (src, dst) in enumerate(
            ((k_hbm, slot(0, c, 2)), (v_hbm, slot(1, c, 2)), (q_hbm, qbuf.at[c]), (g_hbm, gbuf.at[c]))
        ):
            out.append(pltpu.make_async_copy(part(src, c), dst, own_sem.at[c, i]))
        return out

    def remote(src, dst, send, recv, target):
        return pltpu.make_async_remote_copy(
            src_ref=src, dst_ref=dst, send_sem=send, recv_sem=recv,
            device_id={"seq": target}, device_id_type=MESH,
        )

    def kv_copy(kind, a, c):
        dst_slot = (1, 3, 0, 0)[kind]
        target = (d + 1, d - 1, d + 2, d + 1)[kind]
        src = slot(a, c, 1) if kind == 3 else part(hbm[a], c)
        return remote(
            src, slot(a, c, dst_slot), kv_send.at[c, kind, a],
            kv_recv.at[c, (0, 1, 0, 2)[dst_slot], a], target,
        )

    has_prev = d >= 1
    has_prev2 = d >= 2
    has_next = d + 1 < n
    has_next2 = d + 2 < n
    kv_cond = (has_next, has_prev, even & has_next2, even & has_prev2)
    in_cond = (has_prev2, has_prev, has_next)

    def kv_arrived(place, a, c):
        s = (0, 1, 3)[place]
        return remote(slot(a, c, s), slot(a, c, s), kv_send.at[c, 0, a], kv_recv.at[c, place, a], d)

    def gr_copy(kind, to_place, target, a, c):
        return remote(
            gsend.at[c, kind, a], grecv.at[c, to_place, a], gr_send.at[c, kind, a],
            gr_recv.at[c, to_place, a], target,
        )

    barrier = pltpu.get_barrier_semaphore()
    peers = (
        (has_prev, d - 1), (has_next, d + 1),
        (even & has_prev2, d - 2), (even & has_next2, d + 2),
    )
    total = 0
    for cond, target in peers:
        total = total + cond.astype(jnp.int32)

        @pl.when(cond)
        def _(target=target):
            pl.semaphore_signal(barrier, inc=1, device_id={"seq": target}, device_id_type=MESH)

    def start_own(c, carry):
        for copy in own_copies(c):
            copy.start()
        return carry

    lax.fori_loop(0, NCH, start_own, 0)
    pl.semaphore_wait(barrier, total)

    def start_kv(c, carry):
        for kind in (2, 0, 1):
            @pl.when(kv_cond[kind])
            def _(kind=kind):
                for a in range(2):
                    kv_copy(kind, a, c).start()
        return carry

    lax.fori_loop(0, NCH, start_kv, 0)

    for place, s in ((0, 0), (1, 1), (2, 3)):
        @pl.when(jnp.logical_not(in_cond[place]))
        def _(s=s):
            for a in range(2):
                for c in range(NCH):
                    bufs[a][c, pl.ds(s * rows, rows), :] = jnp.zeros((rows, cols), BF)

    position = lax.broadcasted_iota(jnp.int32, (BLK, BLK), 0)
    first = d * blocks
    for e in range(4 * blocks):
        index = first - 2 * blocks + e
        inside = (index >= 0) & (index < nblk)
        count = counts_ref[jnp.clip(index, 0, nblk - 1)]
        for a in range(blocks):
            listed = local_ref[first + a, 0] == index
            for s in range(1, local_ref.shape[1]):
                listed = listed | (local_ref[first + a, s] == index)
            for s in range(far_ref.shape[1]):
                listed = listed | (far_ref[first + a, s] == index)
            live = jnp.where(listed & inside, count, 0)
            bias[pl.ds(e * BLK, BLK), pl.ds(a * BLK, BLK)] = jnp.where(position < live, 0.0, OFF)

    def compute(c):
        done = set()
        for h in range(hpc):
            low = h * head
            w0 = low // 128 * 128
            w1 = -(-(low + head) // 128) * 128
            w = w1 - w0
            lane = lax.broadcasted_iota(jnp.int32, (1, w), 1) + w0
            inhead = ((lane >= low) & (lane < low + head)).astype(F32)
            inhead_b = inhead.astype(BF)
            win = pl.ds(w0, w)
            qm = qbuf[c, :, win] * inhead_b
            gm = gbuf[c, :, win] * inhead_b
            kw = kbuf[c, :, win]
            vw = vbuf[c, :, win]
            s = dot_nt(kw, qm) * (scale * math.log2(math.e)) + bias[...]
            peak = jnp.max(s, axis=0, keepdims=True)
            e = jnp.exp2(s - peak)
            inv = 1.0 / jnp.sum(e, axis=0, keepdims=True)
            p = e * inv
            dp = dot_nt(vw, gm)
            delta = jnp.sum(p * dp, axis=0, keepdims=True)
            pb = p.astype(BF)
            ds = (p * (dp - delta)).astype(BF)
            terms = (
                (oacc, 0, dot_tn(pb, vw) * inhead),
                (oacc, 1, dot_tn(ds, kw) * inhead),
                (acc, 0, dot_nn(ds, qm)),
                (acc, 1, dot_nn(pb, gm)),
            )
            for ref, i, term in terms:
                for t in range(w0, w1, 128):
                    piece = term[:, t - w0 : t - w0 + 128]
                    at = pl.ds(t, 128)
                    if t in done:
                        ref[i, :, at] += piece
                    else:
                        ref[i, :, at] = piece
            done.update(range(w0, w1, 128))
        at = pl.ds(pl.multiple_of(c * cols, 128), cols)
        o_ref[:, at] = oacc[0].astype(BF)
        dq_ref[:, at] = (oacc[1] * scale).astype(BF)
        for a in range(2):
            f = scale if a == 0 else 1.0
            for kind, s in ((0, 0), (1, 1), (2, 3)):
                gsend[c, kind, a] = (acc[a, pl.ds(s * rows, rows), :] * f).astype(BF)
            own[c, a] = acc[a, pl.ds(2 * rows, rows), :] * f

    def chunk(c, carry):
        @pl.when(has_prev)
        def _():
            for a in range(2):
                kv_arrived(1, a, c).wait_recv()

        @pl.when(kv_cond[3])
        def _():
            for a in range(2):
                kv_copy(3, a, c).start()

        for place in (0, 2):
            @pl.when(in_cond[place])
            def _(place=place):
                for a in range(2):
                    kv_arrived(place, a, c).wait_recv()

        for copy in own_copies(c):
            copy.wait()
        compute(c)

        @pl.when(even)
        def _():
            for a in range(2):
                @pl.when(has_prev2)
                def _(a=a):
                    gr_copy(0, 0, d - 2, a, c).start()
                gr_copy(2, 2, d + 1, a, c).start()

            @pl.when(has_prev2)
            def _():
                for a in range(2):
                    gr_copy(0, 3, d, a, c).wait_recv()
                    gsend[c, 1, a] = (
                        gsend[c, 1, a].astype(F32) + grecv[c, 3, a].astype(F32)
                    ).astype(BF)
                    gr_copy(1, 1, d - 1, a, c).start()

        @pl.when(jnp.logical_not(even))
        def _():
            @pl.when(has_prev2)
            def _():
                for a in range(2):
                    gr_copy(0, 3, d - 1, a, c).start()

            @pl.when(has_next)
            def _():
                for a in range(2):
                    gr_copy(2, 2, d + 1, a, c).start()
            for a in range(2):
                gr_copy(1, 1, d - 1, a, c).start()

        return carry

    lax.fori_loop(0, NCH, chunk, 0)

    def finish(c, carry):
        at = pl.ds(pl.multiple_of(c * cols, 128), cols)
        for place, cond in ((2, has_prev), (0, even & has_next2), (1, has_next)):
            @pl.when(cond)
            def _(place=place):
                for a in range(2):
                    gr_copy(0, place, d, a, c).wait_recv()
                    own[c, a] += grecv[c, place, a].astype(F32)
        dk_ref[:, at] = own[c, 0].astype(BF)
        dv_ref[:, at] = own[c, 1].astype(BF)
        for kind in range(4):
            @pl.when(kv_cond[kind])
            def _(kind=kind):
                for a in range(2):
                    kv_copy(kind, a, c).wait_send()
        for kind, cond in ((0, has_prev2), (1, has_prev), (2, has_next)):
            @pl.when(cond)
            def _(kind=kind):
                for a in range(2):
                    gr_copy(kind, kind, d, a, c).wait_send()
        return carry

    lax.fori_loop(0, NCH, finish, 0)


def body(queries, keys, values, cotangent, local_blocks, far_blocks, counts):
    rows, width = queries.shape
    cols = width // NCH
    n = lax.axis_size("seq")
    window = 4 * rows
    out = jax.ShapeDtypeStruct((rows, width), BF)
    any_spec = pl.BlockSpec(memory_space=pl.ANY)
    vmem = pl.BlockSpec(memory_space=pltpu.VMEM)
    smem = pl.BlockSpec(memory_space=pltpu.SMEM)
    dma = pltpu.SemaphoreType.DMA
    return pl.pallas_call(
        functools.partial(kernel, n),
        out_shape=(out,) * 4,
        in_specs=[any_spec] * 4 + [smem] * 3,
        out_specs=(vmem,) * 4,
        scratch_shapes=[
            pltpu.VMEM((NCH, window, cols), BF),
            pltpu.VMEM((NCH, window, cols), BF),
            pltpu.VMEM((NCH, rows, cols), BF),
            pltpu.VMEM((NCH, rows, cols), BF),
            pltpu.VMEM((window, rows), F32),
            pltpu.VMEM((2, window, cols), F32),
            pltpu.VMEM((NCH, 2, rows, cols), F32),
            pltpu.VMEM((2, rows, cols), F32),
            pltpu.VMEM((NCH, 3, 2, rows, cols), BF),
            pltpu.VMEM((NCH, 4, 2, rows, cols), BF),
            dma((NCH, 4)),
            dma((NCH, 4, 2)),
            dma((NCH, 3, 2)),
            dma((NCH, 3, 2)),
            dma((NCH, 4, 2)),
        ],
        compiler_params=pltpu.CompilerParams(
            collective_id=0, has_side_effects=True, vmem_limit_bytes=56 * 1024 * 1024
        ),
        name="attention",
    )(queries, keys, values, cotangent, local_blocks, far_blocks, counts)


def solution(mesh):
    rows = P(("groups", "seq"), None)
    return jax.shard_map(
        body,
        mesh=mesh,
        in_specs=(rows, rows, rows, rows, P("groups", None), P("groups", None), P("groups")),
        out_specs=(rows,) * 4,
        check_vma=False,
    )
```

profile of v0, /device:TPU:9, one launch (start us, length us, event | category | flops | bytes accessed | tf_op | source)
XLA Modules:
  0.0 100.0 jit_solution(6796676350503704541)
XLA Ops:
  0.6 0.0 copy-start.3
  0.6 1.4 %copy.11.local_ref = s32[32,3]{1,0:T(8,128)} copy(s32[32,3]{0,1:T(4,128)} %param.11) | data formatting | bytes 768 | tf_op args[4]
  2.0 0.0 copy-done.3
  2.0 0.7 copy.12.far_ref
  2.7 91.8 %attention.1 = (bf16[256,1280]{1,0:T(8,128)(2,1)}, bf16[256,1280]{1,0:T(8,128)(2,1)}, bf16[256,1280]{1,0:T(8,128)(2,1)}, bf16[256,1280]{1,0:T(8,128)(2,1)}) custom-call(bf16[256,1280]{1,0:T(8,128)(2,1)} %q_hbm.1, bf16[256,1280]{1,0:T(8,128)(2,1)} %k_hbm.1, bf16[256,1280]{1,0:T(8,128)(2,1)} %v_hbm.1, bf16[256,1280]{1,0:T(8,128)(2,1)} %g_hbm.1, ...), custom_call_target="tpu_custom_call" | custom-call | tf_op jit(solution)/shard_map/attention/pallas_call | solution.py:288
  94.5 0.0 copy-start.2
  94.5 2.0 %copy.17 = bf16[256,1280]{1,0:T(8,128)(2,1)} copy(bf16[256,1280]{1,0:T(8,128)(2,1)} %get-tuple-element.8) | data formatting | bytes 1310720
  96.5 0.0 copy-done.2
  96.5 0.0 copy-start.1
  96.5 0.8 copy.18
  97.4 0.5 copy-done.1
  97.9 0.0 copy-start
  97.9 0.8 copy.19
  98.7 0.5 copy-done
  99.2 0.8 copy.20
Async XLA Ops:
  0.6 1.4 %copy-start.3 = (s32[32,4]{0,1:T(4,128)S(1)}, s32[32,4]{0,1:T(4,128)}, u32[]{:S(2)}) copy-start(s32[32,4]{0,1:T(4,128)} %param.12) | copy-start | bytes 1540
  94.5 2.0 %copy-start.2 = (bf16[256,1280]{1,0:T(8,128)(2,1)S(1)}, bf16[256,1280]{1,0:T(8,128)(2,1)}, u32[]{:S(2)}) copy-start(bf16[256,1280]{1,0:T(8,128)(2,1)} %get-tuple-element.9) | copy-start | bytes 1966084
  96.5 1.3 %copy-start.1 = (bf16[256,1280]{1,0:T(8,128)(2,1)S(1)}, bf16[256,1280]{1,0:T(8,128)(2,1)}, u32[]{:S(2)}) copy-start(bf16[256,1280]{1,0:T(8,128)(2,1)} %get-tuple-element.10) | copy-start | bytes 1966084
  97.9 1.3 %copy-start = (bf16[256,1280]{1,0:T(8,128)(2,1)S(1)}, bf16[256,1280]{1,0:T(8,128)(2,1)}, u32[]{:S(2)}) copy-start(bf16[256,1280]{1,0:T(8,128)(2,1)} %get-tuple-element.11) | copy-start | bytes 1966084
where the time goes:
time: 100 us
  Pallas kernels  91.8 us (92%)
  local copies, waits for them, and re-layouts  7.58 us (8%)
    pallas_call x1, Pallas kernels, body(): pl.pallas_call(functools.partial(kernel, n), out_shape=(out,) * 4, in_spe...  91.8 us
    unnamed x14, local copies, waits for them, and re-layouts  7.58 us

commit v1 on v0

v1 whole, which is shorter than its diff:
```python
import functools
import math

import jax
import jax.numpy as jnp
from jax import lax
from jax.experimental import pallas as pl
from jax.experimental.pallas import tpu as pltpu
from jax.sharding import PartitionSpec as P

HEADS = 16
BLK = 128
MESH = pl.DeviceIdType.MESH
OFF = -1e30
NCH = 2
BF = jnp.bfloat16
F32 = jnp.float32


def dot_nt(a, b):
    return lax.dot_general(a, b, (((1,), (1,)), ((), ())), preferred_element_type=F32)


def dot_nn(a, b):
    return lax.dot_general(a, b, (((1,), (0,)), ((), ())), preferred_element_type=F32)


def dot_tn(a, b):
    return lax.dot_general(a, b, (((0,), (0,)), ((), ())), preferred_element_type=F32)


def kernel(
    n, q_hbm, k_hbm, v_hbm, g_hbm, local_ref, far_ref, counts_ref,
    o_ref, dq_ref, dk_ref, dv_ref,
    kbuf, vbuf, qbuf, gbuf, bias, acc, own, oacc, gsend, grecv,
    transit, own_sem, kv_send, kv_recv, gr_send, gr_recv,
):
    d = lax.axis_index("seq")
    place4 = lax.rem(d, 4)
    r0, r1, r2, r3 = (place4 == i for i in range(4))
    even = r0 | r2
    odd = r1 | r3
    rows, width = q_hbm.shape
    cols = width // NCH
    head = width // HEADS
    hpc = HEADS // NCH
    blocks = rows // BLK
    nblk = counts_ref.shape[0]
    hbm = (k_hbm, v_hbm)
    bufs = (kbuf, vbuf)
    scale = 1.0 / math.sqrt(head)
    early = 4
    cut = -(-(early * head) // 128) * 128
    spans = ((0, cut), (cut, cols - cut))

    def slot(a, c, s):
        return bufs[a].at[c, pl.ds(s * rows, rows), :]

    def span(ref, p):
        return ref.at[:, pl.ds(spans[p][0], spans[p][1])]

    def part(ref, c, p):
        return ref.at[:, pl.ds(pl.multiple_of(c * cols + spans[p][0], 128), spans[p][1])]

    def own_copies(c, p):
        out = []
        for i, (src, dst) in enumerate(
            ((k_hbm, slot(0, c, 2)), (v_hbm, slot(1, c, 2)), (q_hbm, qbuf.at[c]), (g_hbm, gbuf.at[c]))
        ):
            out.append(pltpu.make_async_copy(part(src, c, p), span(dst, p), own_sem.at[c, p, i]))
        return out

    def remote(src, dst, send, recv, delta):
        return pltpu.make_async_remote_copy(
            src_ref=src, dst_ref=dst, send_sem=send, recv_sem=recv,
            device_id={"seq": d + delta}, device_id_type=MESH,
        )

    def landing(place, a, c, p):
        return span(transit.at[c, a] if place == 3 else slot(a, c, (0, 1, 3)[place]), p)

    def kv_send_all(kind, src_place, dst_place, delta, c, p):
        for a in range(2):
            src = part(hbm[a], c, p) if src_place is None else landing(src_place, a, c, p)
            remote(
                src, landing(dst_place, a, c, p), kv_send.at[c, p, kind, a],
                kv_recv.at[c, p, dst_place, a], delta,
            ).start()

    def kv_wait(place, c, p):
        for a in range(2):
            there = landing(place, a, c, p)
            remote(there, there, kv_send.at[c, p, 0, a], kv_recv.at[c, p, place, a], 0).wait_recv()

    def kv_wait_send(kind, c, p):
        for a in range(2):
            there = landing(0, a, c, p)
            remote(there, there, kv_send.at[c, p, kind, a], kv_recv.at[c, p, 0, a], 0).wait_send()

    def gr_send_all(kind, place, delta, c, p):
        for a in range(2):
            src = grecv.at[c, 2, a] if kind == 3 else gsend.at[c, kind, a]
            remote(
                span(src, p), span(grecv.at[c, place, a], p), gr_send.at[c, p, kind, a],
                gr_recv.at[c, p, place, a], delta,
            ).start()

    def gr_wait(place, c, p):
        for a in range(2):
            there = span(grecv.at[c, place, a], p)
            remote(there, there, gr_send.at[c, p, 0, a], gr_recv.at[c, p, place, a], 0).wait_recv()

    def gr_wait_send(kind, c, p):
        for a in range(2):
            there = span(grecv.at[c, 0, a], p)
            remote(there, there, gr_send.at[c, p, kind, a], gr_recv.at[c, p, 0, a], 0).wait_send()

    has_prev = d >= 1
    has_prev2 = d >= 2
    has_next = d + 1 < n
    low4 = d >= 4
    up4 = d + 4 < n
    up3 = d + 3 < n
    in_cond = (has_prev2, has_prev, has_next)
    k2_cond = (r0 & up4) | (r1 & up3) | (r2 & low4)
    k3_cond = (r0 & low4) | r2
    kv_cond = (even | odd, jnp.logical_not(r3) | has_next, k2_cond, k3_cond)

    barrier = pltpu.get_barrier_semaphore()
    total = 0
    for delta, who in (
        (1, r0 | r1 | r2), (-1, r1 | r2 | r3), (2, r0), (-2, r2),
        (3, r0 | r1 | r3), (-3, r0 | r2 | r3), (4, r0), (-4, r0),
    ):
        cond = who & (d + delta >= 0) & (d + delta < n)
        total = total + cond.astype(jnp.int32)

        @pl.when(cond)
        def _(delta=delta):
            pl.semaphore_signal(barrier, inc=1, device_id={"seq": d + delta}, device_id_type=MESH)

    def start_own(c, carry):
        for p in range(2):
            for copy in own_copies(c, p):
                copy.start()
        return carry

    lax.fori_loop(0, NCH, start_own, 0)
    pl.semaphore_wait(barrier, total)

    def start_kv(c, carry):
        for p in range(2):
            pl.when(r0)(lambda: kv_send_all(1, None, 0, 2, c, p))
            pl.when(r1)(lambda: kv_send_all(1, None, 1, 1, c, p))
            pl.when(r2)(lambda: kv_send_all(1, None, 2, -1, c, p))
            pl.when(r3 & has_next)(lambda: kv_send_all(1, None, 3, -3, c, p))
            pl.when(even)(lambda: kv_send_all(0, None, 1, 1, c, p))
            pl.when(odd)(lambda: kv_send_all(0, None, 2, -1, c, p))
        return carry

    lax.fori_loop(0, NCH, start_kv, 0)

    def hand_on(c, p):
        @pl.when(r0 & up4)
        def _():
            kv_wait(3, c, p)
            kv_send_all(2, 3, 1, 4, c, p)

        @pl.when(r1)
        def _():
            kv_wait(2, c, p)
            pl.when(up3)(lambda: kv_send_all(2, 2, 0, 3, c, p))

        @pl.when(r2)
        def _():
            kv_wait(0, c, p)
            pl.when(low4)(lambda: kv_send_all(2, 0, 2, -3, c, p))
            kv_wait(1, c, p)
            kv_send_all(3, 1, 0, 1, c, p)

    def arrive(c, p):
        @pl.when(r0 & low4)
        def _():
            kv_wait(1, c, p)
            kv_send_all(3, 1, 0, 1, c, p)
            kv_wait(0, c, p)
        pl.when(even)(lambda: kv_wait(2, c, p))
        pl.when(odd)(lambda: kv_wait(1, c, p))
        pl.when(odd & has_prev2)(lambda: kv_wait(0, c, p))
        pl.when(r3 & has_next)(lambda: kv_wait(2, c, p))
        for copy in own_copies(c, p):
            copy.wait()

    def add_in(kind, place, c, p):
        at = pl.ds(spans[p][0], spans[p][1])
        gr_wait(place, c, p)
        for a in range(2):
            gsend[c, kind, a, :, at] = (
                gsend[c, kind, a, :, at].astype(F32) + grecv[c, place, a, :, at].astype(F32)
            ).astype(BF)

    def emit(c, p):
        at = pl.ds(spans[p][0], spans[p][1])
        for a in range(2):
            f = scale if a == 0 else 1.0
            for kind, s in ((0, 0), (1, 1), (2, 3)):
                gsend[c, kind, a, :, at] = (acc[a, pl.ds(s * rows, rows), at] * f).astype(BF)
            own[c, a, :, at] = acc[a, pl.ds(2 * rows, rows), at] * f
        pl.when(r0 & low4)(lambda: gr_send_all(0, 2, -3, c, p))
        pl.when(odd & has_prev2)(lambda: gr_send_all(0, 3, -1, c, p))
        pl.when(r3 & has_next)(lambda: gr_send_all(2, 2, 3, c, p))
        pl.when(even)(lambda: gr_send_all(2, 0, 1, c, p))
        pl.when(odd)(lambda: gr_send_all(1, 0, -1, c, p))

    def combine(c, p):
        @pl.when(r0 & low4)
        def _():
            add_in(1, 3, c, p)
            gr_send_all(1, 2, -4, c, p)

        @pl.when(r1)
        def _():
            pl.when(up3)(lambda: add_in(2, 2, c, p))
            gr_send_all(2, 1, 1, c, p)

        @pl.when(r2)
        def _():
            add_in(1, 3, c, p)
            gr_send_all(1, 1, -1, c, p)
            pl.when(low4)(lambda: add_in(0, 2, c, p))
            gr_send_all(0, 1, -2, c, p)

    def pass_back(c, p):
        @pl.when(r0 & up4)
        def _():
            gr_wait(2, c, p)
            gr_send_all(3, 1, 3, c, p)

    hand_on(0, 0)

    for place, s in ((0, 0), (1, 1), (2, 3)):
        @pl.when(jnp.logical_not(in_cond[place]))
        def _(s=s):
            for a in range(2):
                for c in range(NCH):
                    bufs[a][c, pl.ds(s * rows, rows), :] = jnp.zeros((rows, cols), BF)

    position = lax.broadcasted_iota(jnp.int32, (BLK, BLK), 0)
    first = d * blocks
    for e in range(4 * blocks):
        index = first - 2 * blocks + e
        inside = (index >= 0) & (index < nblk)
        count = counts_ref[jnp.clip(index, 0, nblk - 1)]
        for a in range(blocks):
            listed = local_ref[first + a, 0] == index
            for s in range(1, local_ref.shape[1]):
                listed = listed | (local_ref[first + a, s] == index)
            for s in range(far_ref.shape[1]):
                listed = listed | (far_ref[first + a, s] == index)
            live = jnp.where(listed & inside, count, 0)
            bias[pl.ds(e * BLK, BLK), pl.ds(a * BLK, BLK)] = jnp.where(position < live, 0.0, OFF)

    hand_on(0, 1)

    def compute(c):
        done = set()
        for h in range(hpc):
            if h == 0:
                arrive(c, 0)
            if h == early:
                pl.when(c == 0)(lambda: hand_on(1, 0))
                pl.when(c == 1)(lambda: combine(0, 0))
                arrive(c, 1)
            if h == early + 1:
                emit(c, 0)
                pl.when(c == 0)(lambda: hand_on(1, 1))

                @pl.when(c == 1)
                def _():
                    combine(0, 1)
                    pass_back(0, 0)
            low = h * head
            w0 = low // 128 * 128
            w1 = -(-(low + head) // 128) * 128
            w = w1 - w0
            lane = lax.broadcasted_iota(jnp.int32, (1, w), 1) + w0
            inhead = ((lane >= low) & (lane < low + head)).astype(F32)
            inhead_b = inhead.astype(BF)
            win = pl.ds(w0, w)
            qm = qbuf[c, :, win] * inhead_b
            gm = gbuf[c, :, win] * inhead_b
            kw = kbuf[c, :, win]
            vw = vbuf[c, :, win]
            s = dot_nt(kw, qm) * (scale * math.log2(math.e)) + bias[...]
            peak = jnp.max(s, axis=0, keepdims=True)
            e = jnp.exp2(s - peak)
            inv = 1.0 / jnp.sum(e, axis=0, keepdims=True)
            p = e * inv
            dp = dot_nt(vw, gm)
            delta = jnp.sum(p * dp, axis=0, keepdims=True)
            pb = p.astype(BF)
            ds = (p * (dp - delta)).astype(BF)
            terms = (
                (oacc, 0, dot_tn(pb, vw) * inhead),
                (oacc, 1, dot_tn(ds, kw) * inhead),
                (acc, 0, dot_nn(ds, qm)),
                (acc, 1, dot_nn(pb, gm)),
            )
            for ref, i, term in terms:
                for t in range(w0, w1, 128):
                    piece = term[:, t - w0 : t - w0 + 128]
                    at = pl.ds(t, 128)
                    if t in done:
                        ref[i, :, at] += piece
                    else:
                        ref[i, :, at] = piece
            done.update(range(w0, w1, 128))
        at = pl.ds(pl.multiple_of(c * cols, 128), cols)
        o_ref[:, at] = oacc[0].astype(BF)
        dq_ref[:, at] = (oacc[1] * scale).astype(BF)

    def chunk(c, carry):
        compute(c)
        emit(c, 1)
        return carry

    lax.fori_loop(0, NCH, chunk, 0)

    combine(1, 0)
    pass_back(0, 1)
    combine(1, 1)
    pass_back(1, 0)

    def finish(c, carry):
        pl.when(c == 1)(lambda: pass_back(1, 1))
        at = pl.ds(pl.multiple_of(c * cols, 128), cols)
        for p in range(2):
            gr_wait(0, c, p)
            pl.when(jnp.logical_not(r3) | has_next)(lambda: gr_wait(1, c, p))
        for a, ref in ((0, dk_ref), (1, dv_ref)):
            mine = own[c, a] + grecv[c, 0, a].astype(F32)
            other = grecv[c, 1, a].astype(F32)
            ref[:, at] = (mine + jnp.where(jnp.logical_not(r3) | has_next, other, 0.0)).astype(BF)
        for p in range(2):
            for kind in range(4):
                pl.when(kv_cond[kind])(lambda: kv_wait_send(kind, c, p))
            for kind, cond in ((0, has_prev2), (1, has_prev), (2, has_next), (3, r0 & up4)):
                pl.when(cond)(lambda: gr_wait_send(kind, c, p))
        return carry

    lax.fori_loop(0, NCH, finish, 0)


def body(queries, keys, values, cotangent, local_blocks, far_blocks, counts):
    rows, width = queries.shape
    cols = width // NCH
    n = lax.axis_size("seq")
    window = 4 * rows
    out = jax.ShapeDtypeStruct((rows, width), BF)
    any_spec = pl.BlockSpec(memory_space=pl.ANY)
    vmem = pl.BlockSpec(memory_space=pltpu.VMEM)
    smem = pl.BlockSpec(memory_space=pltpu.SMEM)
    dma = pltpu.SemaphoreType.DMA
    return pl.pallas_call(
        functools.partial(kernel, n),
        out_shape=(out,) * 4,
        in_specs=[any_spec] * 4 + [smem] * 3,
        out_specs=(vmem,) * 4,
        scratch_shapes=[
            pltpu.VMEM((NCH, window, cols), BF),
            pltpu.VMEM((NCH, window, cols), BF),
            pltpu.VMEM((NCH, rows, cols), BF),
            pltpu.VMEM((NCH, rows, cols), BF),
            pltpu.VMEM((window, rows), F32),
            pltpu.VMEM((2, window, cols), F32),
            pltpu.VMEM((NCH, 2, rows, cols), F32),
            pltpu.VMEM((2, rows, cols), F32),
            pltpu.VMEM((NCH, 3, 2, rows, cols), BF),
            pltpu.VMEM((NCH, 4, 2, rows, cols), BF),
            pltpu.VMEM((NCH, 2, rows, cols), BF),
            dma((NCH, 2, 4)),
            dma((NCH, 2, 4, 2)),
            dma((NCH, 2, 4, 2)),
            dma((NCH, 2, 4, 2)),
            dma((NCH, 2, 4, 2)),
        ],
        compiler_params=pltpu.CompilerParams(
            collective_id=0, has_side_effects=True, vmem_limit_bytes=56 * 1024 * 1024
        ),
        name="attention",
    )(queries, keys, values, cotangent, local_blocks, far_blocks, counts)


def solution(mesh):
    rows = P(("groups", "seq"), None)
    return jax.shard_map(
        body,
        mesh=mesh,
        in_specs=(rows, rows, rows, rows, P("groups", None), P("groups", None), P("groups")),
        out_specs=(rows,) * 4,
        check_vma=False,
    )
```

time: 100 us -> 90 us (0.900)
  the two profiles are of different devices: /device:TPU:9 before, /device:TPU:21 now
where the time goes in v1:
time: 90 us; the launch traced here: 89 us
  Pallas kernels  80.8 us (90%)
  local copies, waits for them, and re-layouts  7.58 us (8%)
    pallas_call x1, Pallas kernels, body(): pl.pallas_call(functools.partial(kernel, n), out_shape=(out,) * 4, in_spe...  80.8 us
    unnamed x14, local copies, waits for them, and re-layouts  7.58 us

profile of v1, /device:TPU:21, one launch (start us, length us, event | category | flops | bytes accessed | tf_op | source)
XLA Modules:
  0.0 89.0 jit_solution(17989756451402561169)
XLA Ops:
  0.6 0.0 copy-start.3
  0.6 1.4 %copy.11.local_ref = s32[32,3]{1,0:T(8,128)} copy(s32[32,3]{0,1:T(4,128)} %param.11) | data formatting | bytes 768 | tf_op args[4]
  2.0 0.0 copy-done.3
  2.0 0.7 copy.12.far_ref
  2.7 80.8 %attention.1 = (bf16[256,1280]{1,0:T(8,128)(2,1)}, bf16[256,1280]{1,0:T(8,128)(2,1)}, bf16[256,1280]{1,0:T(8,128)(2,1)}, bf16[256,1280]{1,0:T(8,128)(2,1)}) custom-call(bf16[256,1280]{1,0:T(8,128)(2,1)} %q_hbm.1, bf16[256,1280]{1,0:T(8,128)(2,1)} %k_hbm.1, bf16[256,1280]{1,0:T(8,128)(2,1)} %v_hbm.1, bf16[256,1280]{1,0:T(8,128)(2,1)} %g_hbm.1, ...), custom_call_target="tpu_custom_call" | custom-call | tf_op jit(solution)/shard_map/attention/pallas_call | solution.py:364
  83.5 0.0 copy-start.2
  83.5 2.0 %copy.17 = bf16[256,1280]{1,0:T(8,128)(2,1)} copy(bf16[256,1280]{1,0:T(8,128)(2,1)} %get-tuple-element.8) | data formatting | bytes 1310720
  85.6 0.0 copy-done.2
  85.6 0.0 copy-start.1
  85.6 0.8 copy.18
  86.4 0.5 copy-done.1
  86.9 0.0 copy-start
  86.9 0.8 copy.19
  87.7 0.5 copy-done
  88.2 0.8 copy.20
Async XLA Ops:
  0.6 1.4 %copy-start.3 = (s32[32,4]{0,1:T(4,128)S(1)}, s32[32,4]{0,1:T(4,128)}, u32[]{:S(2)}) copy-start(s32[32,4]{0,1:T(4,128)} %param.12) | copy-start | bytes 1540
  83.5 2.0 %copy-start.2 = (bf16[256,1280]{1,0:T(8,128)(2,1)S(1)}, bf16[256,1280]{1,0:T(8,128)(2,1)}, u32[]{:S(2)}) copy-start(bf16[256,1280]{1,0:T(8,128)(2,1)} %get-tuple-element.9) | copy-start | bytes 1966084
  85.6 1.3 %copy-start.1 = (bf16[256,1280]{1,0:T(8,128)(2,1)S(1)}, bf16[256,1280]{1,0:T(8,128)(2,1)}, u32[]{:S(2)}) copy-start(bf16[256,1280]{1,0:T(8,128)(2,1)} %get-tuple-element.10) | copy-start | bytes 1966084
  86.9 1.3 %copy-start = (bf16[256,1280]{1,0:T(8,128)(2,1)S(1)}, bf16[256,1280]{1,0:T(8,128)(2,1)}, u32[]{:S(2)}) copy-start(bf16[256,1280]{1,0:T(8,128)(2,1)} %get-tuple-element.11) | copy-start | bytes 1966084

commit v2 on v1

--- a/solution.py
+++ b/solution.py
@@ -212,12 +212,18 @@
         pl.when(even)(lambda: gr_send_all(2, 0, 1, c, p))
         pl.when(odd)(lambda: gr_send_all(1, 0, -1, c, p))
 
-    def combine(c, p):
+    def combine_core(c, p):
         @pl.when(r0 & low4)
         def _():
             add_in(1, 3, c, p)
             gr_send_all(1, 2, -4, c, p)
 
+        @pl.when(r2)
+        def _():
+            add_in(1, 3, c, p)
+            gr_send_all(1, 1, -1, c, p)
+
+    def combine_chip(c, p):
         @pl.when(r1)
         def _():
             pl.when(up3)(lambda: add_in(2, 2, c, p))
@@ -225,8 +231,6 @@
 
         @pl.when(r2)
         def _():
-            add_in(1, 3, c, p)
-            gr_send_all(1, 1, -1, c, p)
             pl.when(low4)(lambda: add_in(0, 2, c, p))
             gr_send_all(0, 1, -2, c, p)
 
@@ -252,11 +256,11 @@
         inside = (index >= 0) & (index < nblk)
         count = counts_ref[jnp.clip(index, 0, nblk - 1)]
         for a in range(blocks):
-            listed = local_ref[first + a, 0] == index
-            for s in range(1, local_ref.shape[1]):
-                listed = listed | (local_ref[first + a, s] == index)
-            for s in range(far_ref.shape[1]):
-                listed = listed | (far_ref[first + a, s] == index)
+            listed = local_ref[0, first + a] == index
+            for s in range(1, local_ref.shape[0]):
+                listed = listed | (local_ref[s, first + a] == index)
+            for s in range(far_ref.shape[0]):
+                listed = listed | (far_ref[s, first + a] == index)
             live = jnp.where(listed & inside, count, 0)
             bias[pl.ds(e * BLK, BLK), pl.ds(a * BLK, BLK)] = jnp.where(position < live, 0.0, OFF)
 
@@ -267,18 +271,22 @@
         for h in range(hpc):
             if h == 0:
                 arrive(c, 0)
+            if h == 1:
+                pl.when(c == 1)(lambda: combine_core(0, 1))
+            if h == 2:
+                pl.when(c == 1)(lambda: combine_chip(0, 0))
             if h == early:
                 pl.when(c == 0)(lambda: hand_on(1, 0))
-                pl.when(c == 1)(lambda: combine(0, 0))
+                pl.when(c == 1)(lambda: pass_back(0, 0))
                 arrive(c, 1)
             if h == early + 1:
                 emit(c, 0)
                 pl.when(c == 0)(lambda: hand_on(1, 1))
-
-                @pl.when(c == 1)
-                def _():
-                    combine(0, 1)
-                    pass_back(0, 0)
+                pl.when(c == 1)(lambda: combine_chip(0, 1))
+            if h == early + 2:
+                pl.when(c == 1)(lambda: pass_back(0, 1))
+            if h == early + 3:
+                combine_core(c, 0)
             low = h * head
             w0 = low // 128 * 128
             w1 = -(-(low + head) // 128) * 128
@@ -326,10 +334,10 @@
 
     lax.fori_loop(0, NCH, chunk, 0)
 
-    combine(1, 0)
-    pass_back(0, 1)
-    combine(1, 1)
+    combine_core(1, 1)
+    combine_chip(1, 0)
     pass_back(1, 0)
+    combine_chip(1, 1)
 
     def finish(c, carry):
         pl.when(c == 1)(lambda: pass_back(1, 1))
@@ -388,7 +396,7 @@
             collective_id=0, has_side_effects=True, vmem_limit_bytes=56 * 1024 * 1024
         ),
         name="attention",
-    )(queries, keys, values, cotangent, local_blocks, far_blocks, counts)
+    )(queries, keys, values, cotangent, local_blocks.T, far_blocks.T, counts)
 
 
 def solution(mesh):

time: 90 us -> 83.6 us (0.929)
  Pallas kernels: 80.8 us -> 77.2 us
  local copies, waits for them, and re-layouts: 7.58 us -> 5.52 us
    pallas_call x1, Pallas kernels: 80.8 us -> 77.2 us  [body(): pl.pallas_call(functools.partial(kernel, n), out_shape=(out,) * 4, in_spe...]
    unnamed x14 -> x10, local copies, waits for them, and re-layouts: 7.58 us -> 5.52 us
where the time goes in v2:
time: 83.6 us; the launch traced here: 83.4 us
  Pallas kernels  77.2 us (92%)
  local copies, waits for them, and re-layouts  5.52 us (7%)
    pallas_call x1, Pallas kernels, body(): pl.pallas_call(functools.partial(kernel, n), out_shape=(out,) * 4, in_spe...  77.2 us
    unnamed x10, local copies, waits for them, and re-layouts  5.52 us

profile of v2, /device:TPU:21, one launch (start us, length us, event | category | flops | bytes accessed | tf_op | source)
XLA Modules:
  0.0 83.4 jit_solution(11445957189386944054)
XLA Ops:
  0.6 77.2 %attention.1 = (bf16[256,1280]{1,0:T(8,128)(2,1)}, bf16[256,1280]{1,0:T(8,128)(2,1)}, bf16[256,1280]{1,0:T(8,128)(2,1)}, bf16[256,1280]{1,0:T(8,128)(2,1)}) custom-call(bf16[256,1280]{1,0:T(8,128)(2,1)} %q_hbm.1, bf16[256,1280]{1,0:T(8,128)(2,1)} %k_hbm.1, bf16[256,1280]{1,0:T(8,128)(2,1)} %v_hbm.1, bf16[256,1280]{1,0:T(8,128)(2,1)} %g_hbm.1, ...), custom_call_target="tpu_custom_call" | custom-call | tf_op jit(solution)/shard_map/attention/pallas_call | solution.py:372
  77.8 0.0 copy-start.2
  77.9 2.0 %copy.15 = bf16[256,1280]{1,0:T(8,128)(2,1)} copy(bf16[256,1280]{1,0:T(8,128)(2,1)} %get-tuple-element.8) | data formatting | bytes 1310720
  79.9 0.0 copy-done.2
  79.9 0.0 copy-start.1
  79.9 0.8 %copy.16 = bf16[256,1280]{1,0:T(8,128)(2,1)} copy(bf16[256,1280]{1,0:T(8,128)(2,1)S(1)} %copy-done.2) | data formatting | bytes 1310720
  80.7 0.5 copy-done.1
  81.2 0.0 copy-start
  81.2 0.8 %copy.17 = bf16[256,1280]{1,0:T(8,128)(2,1)} copy(bf16[256,1280]{1,0:T(8,128)(2,1)S(1)} %copy-done.1) | data formatting | bytes 1310720
  82.0 0.5 copy-done
  82.5 0.8 %copy.18 = bf16[256,1280]{1,0:T(8,128)(2,1)} copy(bf16[256,1280]{1,0:T(8,128)(2,1)S(1)} %copy-done) | data formatting | bytes 1310720
Async XLA Ops:
  77.8 2.0 %copy-start.2 = (bf16[256,1280]{1,0:T(8,128)(2,1)S(1)}, bf16[256,1280]{1,0:T(8,128)(2,1)}, u32[]{:S(2)}) copy-start(bf16[256,1280]{1,0:T(8,128)(2,1)} %get-tuple-element.9) | copy-start | bytes 1966084
  79.9 1.3 %copy-start.1 = (bf16[256,1280]{1,0:T(8,128)(2,1)S(1)}, bf16[256,1280]{1,0:T(8,128)(2,1)}, u32[]{:S(2)}) copy-start(bf16[256,1280]{1,0:T(8,128)(2,1)} %get-tuple-element.10) | copy-start | bytes 1966084
  81.2 1.3 %copy-start = (bf16[256,1280]{1,0:T(8,128)(2,1)S(1)}, bf16[256,1280]{1,0:T(8,128)(2,1)}, u32[]{:S(2)}) copy-start(bf16[256,1280]{1,0:T(8,128)(2,1)} %get-tuple-element.11) | copy-start | bytes 1966084
